TPU v7x, 32 devices: a whole 2x2x4 slice. The times are simulated.
32 devices in a mesh: sect: 2 (over y), node: 4 (over z), fn: 2 (over x), sub: 2 (over core).
Axes of the slice: x: 2, y: 2, z: 4, core: 2. Of those that a mesh axis runs over, the one named last changes fastest.
Arguments:
- volume_grad: bfloat16 [2048, 32, 128], P(('sect', 'node', 'fn', 'sub')), parts along dimension 0, may hold values from -0.5 to 0.5
- volume_coords: float32 [2048, 3, 128], P(('sect', 'node', 'fn', 'sub')), parts along dimension 0, may hold values from -2.1366198 to 3
- support: int32 [2048, 32], P(('sect', 'node', 'fn', 'sub')), parts along dimension 0, may hold values from 0 to 31
- control_coords: float32 [64, 3, 128], P(('sect', 'node')), parts along dimension 0, may hold values from -2.1366198 to 3
- neighbours: int32 [64, 4], P(('sect', 'node')), parts along dimension 0, may hold values from 0 to 31
- block_inverse: float32 [64, 128, 128], P(('sect', 'node')), parts along dimension 0, may hold values from -0.09375 to 0.09375
Outputs:
- control_gradient: float32 [64, 32, 128], P(('sect', 'node')), parts along dimension 0
- adjoint: float32 [64, 32, 128], P(('sect', 'node')), parts along dimension 0
There are 2 independent parts, one for each index of `sect`. A program takes and returns all parts, laid end to end along the dimension named above; each array names one. Nothing has to cross between parts.
All inputs are finite; a program needn't handle non-finite values.
Results may differ from a plain program's by a relative error of at most 0.0034.
Values may be sent and summed in bfloat16 or wider, within the bound.
A program may use at most 64 MiB of HBM per device.

v0:
```python
import jax
import jax.numpy as jnp
from jax import lax
from jax.sharding import PartitionSpec as P

SWEEPS = 2


RADIUS = 1.2


def wendland(points, centers):
    diff = points[..., :, :, None] - centers[..., :, None, :]
    dist = jnp.sqrt(jnp.sum(diff * diff, axis=-3))
    ratio = dist / RADIUS
    inside = jnp.maximum(1.0 - ratio, 0.0)
    return (inside**4 * (4.0 * ratio + 1.0)).astype(jnp.bfloat16)


def local(volume_grad, volume_coords, support, control_coords, neighbours, block_inverse):
    all_centers = lax.all_gather(control_coords, "node", axis=0, tiled=True)
    blocks = volume_grad.shape[0]
    funcs = volume_grad.shape[1]
    width = volume_grad.shape[2]
    listed = support.shape[1]
    group = 2
    count = blocks // group
    grads = volume_grad.reshape(count, group, funcs, width)
    coords = volume_coords.reshape(count, group, 3, width)
    lists = support.reshape(count, group, listed)

    def step(total, items):
        block_grads, block_coords, block_lists = items
        centers = all_centers[block_lists]
        tiles_phi = wendland(block_coords[:, None], centers)
        tiles = jnp.einsum(
            "gfi,gkij->gkfj", block_grads, tiles_phi, preferred_element_type=jnp.float32
        )
        total = total.at[block_lists.reshape(-1)].add(tiles.reshape(-1, funcs, width))
        return (total, None)

    empty = jnp.zeros((all_centers.shape[0], funcs, width), jnp.float32)
    partial_value, _ = lax.scan(step, empty, (grads, coords, lists))
    owned = lax.psum_scatter(partial_value, "node", scatter_dimension=0, tiled=True)
    control_gradient = lax.psum(owned, ("fn", "sub"))
    adjoint = jnp.einsum(
        "cfi,cij->cfj", control_gradient, block_inverse, precision=lax.Precision.HIGHEST
    )
    pair_phi = wendland(all_centers[neighbours], control_coords[:, None])
    for sweep in range(SWEEPS):
        values = lax.all_gather(adjoint.astype(jnp.bfloat16), "node", axis=0, tiled=True)
        near = values[neighbours]
        coupling = jnp.einsum("ckfi,ckij->cfj", near, pair_phi, preferred_element_type=jnp.float32)
        adjoint = jnp.einsum(
            "cfi,cij->cfj",
            control_gradient - coupling,
            block_inverse,
            precision=lax.Precision.HIGHEST,
        )
    return (control_gradient, adjoint)


def solution(mesh):
    return jax.shard_map(
        local,
        mesh=mesh,
        in_specs=(
            P(("sect", "node", "fn", "sub"), None, None),
            P(("sect", "node", "fn", "sub"), None, None),
            P(("sect", "node", "fn", "sub"), None),
            P(("sect", "node"), None, None),
            P(("sect", "node"), None),
            P(("sect", "node"), None, None),
        ),
        out_specs=(P(("sect", "node"), None, None), P(("sect", "node"), None, None)),
        check_vma=False,
    )
```

profile of v0, /device:TPU:0, one launch (start us, length us, event | category | flops | bytes accessed | tf_op | source)
XLA Modules:
  0.0 401.6 jit_solution(12092101449089686073)
XLA Ops:
  9.0 15.0 %all_gather.9 = f32[32,3,128]{2,0,1:T(8,128)S(1)} all-gather(f32[8,3,128]{2,0,1:T(8,128)} %param.11), channel_id=1, replica_groups=mesh['sect'=2,'node'=4,'fn'=2,'sub'=2] {'node'}, dimensions={0}, use_global_device_ids=true | all-gather | bytes 61440 | tf_op jit(solution)/shard_map/all_gather | solution.py:21
  24.1 280.2 %while.12 = (s32[]{:T(128)}, f32[32,32,128]{2,1,0:T(8,128)S(1)}, s32[32,2,32]{2,1,0:T(2,128)S(1)}, f32[32,2,3,128]{3,2,1,0:T(4,128)S(1)}, f32[32,3,128]{2,1,0:T(...) while((s32[]{:T(128)}, f32[32,32,128]{2,1,0:T(8,128)S(1)}, s32[32,2,32]{2,1,0:T(2,128)S(1)}, ...), condition=%wide.region_3.4_spmd, body=%wide.region_0.3_spmd.sunk | while | flops 85198208 | bytes 12910689 | solution.py:43
  38.5 3.1 scatter_fusion
  47.2 3.1 scatter_fusion
  56.0 3.1 scatter_fusion
  64.8 3.1 scatter_fusion
  73.5 3.1 scatter_fusion
  82.3 3.1 scatter_fusion
  91.0 3.1 scatter_fusion
  99.8 3.1 scatter_fusion
  108.5 3.1 scatter_fusion
  117.3 3.1 scatter_fusion
  126.0 3.1 scatter_fusion
  134.8 3.1 scatter_fusion
  143.6 3.1 scatter_fusion
  152.3 3.1 scatter_fusion
  161.1 3.1 scatter_fusion
  169.8 3.1 scatter_fusion
  178.6 3.1 scatter_fusion
  306.0 3.4 multiply_reduce_fusion.1
  309.4 18.7 %reduce-scatter.2.cloned.1.call-done = f32[8,32,128]{2,1,0:T(8,128)} async-done(((f32[32,32,128]{2,1,0:T(8,128)}), f32[8,32,128]{2,1,0:T(8,128)}) %reduce-scatter.2.cloned.1.call-update) | async-done | bytes 131088 | tf_op jit(solution)/shard_map/reduce_scatter | solution.py:44
  330.9 29.3 %all-reduce.2.cloned.1.call-done = f32[8,32,128]{2,1,0:T(8,128)} async-done(((f32[8,32,128]{2,1,0:T(8,128)}), f32[8,32,128]{2,1,0:T(8,128)}) %all-reduce.2.cloned.1.call-update) | async-done | bytes 131088 | tf_op jit(solution)/shard_map/psum | solution.py:45
  361.7 13.9 %all_gather.10 = bf16[32,32,128]{2,1,0:T(8,128)(2,1)S(1)} all-gather(bf16[8,32,128]{2,1,0:T(8,128)(2,1)S(1)} %convolution_convert_fusion.1), channel_id=1, replica_groups=mesh['sect'=2,'node'=4,'fn'=2,'sub'=2] {'node'}, dimensions={0}, use_global_device_ids=true | all-gather | bytes 327680 | tf_op jit(solution)/shard_map/all_gather | solution.py:51
  377.9 14.1 %all_gather.11 = bf16[32,32,128]{2,1,0:T(8,128)(2,1)S(1)} all-gather(bf16[8,32,128]{2,1,0:T(8,128)(2,1)S(1)} %convolution_convert_fusion), channel_id=1, replica_groups=mesh['sect'=2,'node'=4,'fn'=2,'sub'=2] {'node'}, dimensions={0}, use_global_device_ids=true | all-gather | bytes 327680 | tf_op jit(solution)/shard_map/all_gather | solution.py:51
  (336 shorter events, 238.3 us)
Async XLA Ops:
  7.2 353.0 %copy-start = (f32[8,128,128]{2,1,0:T(8,128)S(1)}, f32[8,128,128]{2,1,0:T(8,128)}, u32[]{:S(2)}) copy-start(f32[8,128,128]{2,1,0:T(8,128)} %param.13) | copy-start | bytes 1572868
  7.2 321.0 %reduce-scatter.2.cloned.1.call-start = ((), (), s32[]{:S(2)}) async-start(), calls=%async_computation.1 | async-start | bytes 655360 | tf_op jit(solution)/shard_map/reduce_scatter | solution.py:44
  24.1 281.1 %copy-start.3 = (f32[8,3,128]{2,0,1:T(8,128)S(1)}, f32[8,3,128]{2,0,1:T(8,128)}, u32[]{:S(2)}) copy-start(f32[8,3,128]{2,0,1:T(8,128)} %param.11) | copy-start | bytes 36868
  24.1 281.1 %copy-start.4 = (s32[8,4]{0,1:T(4,128)S(1)}, s32[8,4]{0,1:T(4,128)}, u32[]{:S(2)}) copy-start(s32[8,4]{0,1:T(4,128)} %param.12) | copy-start | bytes 388
  304.3 0.8 copy-start.1
  305.1 55.0 %all-reduce.2.cloned.1.call-start = ((), (), s32[]{:S(2)}) async-start(), calls=%async_computation.2 | async-start | bytes 262144 | tf_op jit(solution)/shard_map/psum | solution.py:45
  360.1 32.5 %copy-start.2 = (f32[8,32,128]{2,1,0:T(8,128)S(1)}, f32[8,32,128]{2,1,0:T(8,128)}, u32[]{:S(2)}) copy-start(f32[8,32,128]{2,1,0:T(8,128)} %all-reduce.2.cloned.1.call-done) | copy-start | bytes 393220
Sparse Core Ops, SparseCore 0:
  305.3 22.8 reduce-scatter.1
  330.5 29.6 all-reduce.1
where the time goes:
time: 405 us; the launch traced here: 402 us
  other arithmetic  161 us (40%)
  matrix products  102 us (25%)
  waiting for transfers between devices  48 us (12%)
  blocking collectives  42.9 us (11%)
  local copies, waits for them, and re-layouts  31.8 us (8%)
  between operations  14.2 us (4%)
    scatter-add x32, other arithmetic, step(): total.at[block_lists.reshape(-1)].add(tiles.reshape(-1, funcs, width))  100 us
    dot_general x32, matrix products, step(): jnp.einsum('gfi,gkij->gkfj', block_grads, tiles_phi, preferred_element_ty...  97 us
    reduce_sum x33, other arithmetic, wendland(): dist = jnp.sqrt(jnp.sum(diff * diff, axis=-3))  57.5 us
    psum x1, waiting for transfers between devices, local(): control_gradient = lax.psum(owned, ('fn', 'sub'))  29.3 us
    all_gather x2, blocking collectives, local(): lax.all_gather(adjoint.astype(jnp.bfloat16), 'node', axis=0, tiled=True)  28 us
    gather x32, local copies, waits for them, and re-layouts, step(): centers = all_centers[block_lists]  21 us
    reduce_scatter x1, waiting for transfers between devices, local(): lax.psum_scatter(partial_value, 'node', scatter_dimension=0, tiled=True)  18.7 us
    all_gather x1, blocking collectives, local(): all_centers = lax.all_gather(control_coords, 'node', axis=0, tiled=True)  15 us
  transfers between devices with their start and end apart: 2, of which 2 were waited for; matrix products, arithmetic and copies ran while one was open for 2% of the time, Pallas kernels for 0%

commit v1 on v0

v1 whole, which is shorter than its diff:
```python
import functools

import jax
import jax.numpy as jnp
from jax import lax
from jax.experimental import pallas as pl
from jax.experimental.pallas import tpu as pltpu
from jax.sharding import PartitionSpec as P

SWEEPS = 2


RADIUS = 1.2


DEPTH = 32


def wendland(points, centers):
    diff = points[..., :, :, None] - centers[..., :, None, :]
    dist = jnp.sqrt(jnp.sum(diff * diff, axis=-3))
    ratio = dist / RADIUS
    inside = jnp.maximum(1.0 - ratio, 0.0)
    return (inside**4 * (4.0 * ratio + 1.0)).astype(jnp.bfloat16)


def cut(x, terms):
    pieces = []
    for _ in range(terms):
        piece = lax.reduce_precision(x, 8, 7)
        pieces.append(piece)
        x = x - piece
    return pieces


def factors(points, left):
    high, low = cut(points * (1.0 / RADIUS), 2)
    kept = high + low
    norm = jnp.concatenate(cut(jnp.sum(kept * kept, axis=1, keepdims=True), 3), axis=1)
    one = jnp.ones_like(norm)
    if left:
        rows = [high, low, high, low, norm, one]
    else:
        rows = [-2.0 * high, -2.0 * high, -2.0 * low, -2.0 * low, one, norm]
    used = sum(row.shape[1] for row in rows)
    rows.append(jnp.zeros((points.shape[0], DEPTH - used, points.shape[2]), jnp.float32))
    return jnp.concatenate(rows, axis=1).astype(jnp.bfloat16)


def quarter_phi(square):
    square = jnp.maximum(square, 1e-12)
    ratio = square * lax.rsqrt(square)
    inside = jnp.maximum(1.0 - ratio, 0.0)
    inside = inside * inside
    return (inside * inside * (ratio + 0.25)).astype(jnp.bfloat16)


def gradient_kernel(left_ref, right_ref, grad_ref, weight_ref, out_ref):
    funcs = grad_ref.shape[0]
    width = out_ref.shape[2]
    square = jnp.dot(left_ref[...], right_ref[0], preferred_element_type=jnp.float32)
    phi = quarter_phi(square)
    grads = grad_ref[...]
    scaled = []
    for half in range(2):
        row = jnp.broadcast_to(weight_ref[0, half : half + 1, :], grads.shape)
        scaled.append(grads * row.astype(jnp.bfloat16))
    both = jnp.dot(jnp.concatenate(scaled, 0), phi, preferred_element_type=jnp.float32)
    out_ref[0] = both[:funcs, :width]
    out_ref[1] = both[funcs:, width:]


def partial_gradient(volume_grad, volume_coords, support, all_centers):
    blocks, funcs, width = volume_grad.shape
    control = all_centers.shape[0]
    pairs = control // 2
    points = blocks * width
    left = factors(volume_coords, True).transpose(0, 2, 1).reshape(points, DEPTH)
    right = factors(all_centers, False).reshape(pairs, 2, DEPTH, width)
    right = right.transpose(0, 2, 1, 3).reshape(pairs, DEPTH, 2 * width)
    grads = volume_grad.transpose(1, 0, 2).reshape(funcs, points)
    listed = support[None] == jnp.arange(control, dtype=jnp.int32)[:, None, None]
    counts = 4.0 * jnp.sum(listed.astype(jnp.float32), axis=2)
    weights = jnp.broadcast_to(counts[:, :, None], (control, blocks, width))
    weights = weights.reshape(pairs, 2, points)
    return pl.pallas_call(
        gradient_kernel,
        grid=(pairs,),
        in_specs=[
            pl.BlockSpec((points, DEPTH), lambda i: (0, 0)),
            pl.BlockSpec((1, DEPTH, 2 * width), lambda i: (i, 0, 0)),
            pl.BlockSpec((funcs, points), lambda i: (0, 0)),
            pl.BlockSpec((1, 2, points), lambda i: (i, 0, 0)),
        ],
        out_specs=pl.BlockSpec((2, funcs, width), lambda i: (i, 0, 0)),
        out_shape=jax.ShapeDtypeStruct((control, funcs, width), jnp.float32),
        compiler_params=pltpu.CompilerParams(vmem_limit_bytes=48 << 20),
    )(left, right, grads, weights)


def local(volume_grad, volume_coords, support, control_coords, neighbours, block_inverse):
    all_centers = lax.all_gather(control_coords, "node", axis=0, tiled=True)
    partial_value = partial_gradient(volume_grad, volume_coords, support, all_centers)
    owned = lax.psum_scatter(partial_value, "node", scatter_dimension=0, tiled=True)
    control_gradient = lax.psum(owned, ("fn", "sub"))
    adjoint = jnp.einsum(
        "cfi,cij->cfj", control_gradient, block_inverse, precision=lax.Precision.HIGHEST
    )
    picks = neighbours[:, :, None] == jnp.arange(all_centers.shape[0], dtype=jnp.int32)
    near_coords = jnp.einsum(
        "ckn,ndi->ckdi", picks.astype(jnp.float32), all_centers, precision=lax.Precision.HIGHEST
    )
    pair_phi = wendland(near_coords, control_coords[:, None])
    picks = picks.astype(jnp.bfloat16)
    for sweep in range(SWEEPS):
        values = lax.all_gather(adjoint.astype(jnp.bfloat16), "node", axis=0, tiled=True)
        near = jnp.einsum("ckn,nfi->ckfi", picks, values)
        coupling = jnp.einsum("ckfi,ckij->cfj", near, pair_phi, preferred_element_type=jnp.float32)
        adjoint = jnp.einsum(
            "cfi,cij->cfj",
            control_gradient - coupling,
            block_inverse,
            precision=lax.Precision.HIGHEST,
        )
    return (control_gradient, adjoint)


def solution(mesh):
    return jax.shard_map(
        local,
        mesh=mesh,
        in_specs=(
            P(("sect", "node", "fn", "sub"), None, None),
            P(("sect", "node", "fn", "sub"), None, None),
            P(("sect", "node", "fn", "sub"), None),
            P(("sect", "node"), None, None),
            P(("sect", "node"), None),
            P(("sect", "node"), None, None),
        ),
        out_specs=(P(("sect", "node"), None, None), P(("sect", "node"), None, None)),
        check_vma=False,
    )
```

time: 405 us -> 184 us (0.45)
  other arithmetic: 161 us -> 7.17 us
  matrix products: 102 us -> 5.45 us
  Pallas kernels: 0 us -> 55.4 us
  local copies, waits for them, and re-layouts: 31.8 us -> 9.96 us
    scatter-add x32 -> x0, other arithmetic: 100 us -> none  [step(): total.at[block_lists.reshape(-1)].add(tiles.reshape(-1, funcs, width))]
    dot_general x32 -> x3, matrix products: 97 us -> 0.75 us  [the longest x2 0.54 us: local(): near = jnp.einsum('ckn,nfi->ckfi', picks, values)]
    pallas_call x0 -> x1, Pallas kernels: none -> 55.4 us  [partial_gradient(): pl.pallas_call(gradient_kernel, grid=(pairs,), in_specs=[pl.BlockSpec((po...]
    reduce_sum x33 -> x1, other arithmetic: 57.5 us -> 3.41 us  [wendland(): dist = jnp.sqrt(jnp.sum(diff * diff, axis=-3))]
    gather x35 -> x0, local copies, waits for them, and re-layouts: 22.8 us -> none  [the longest x32 21 us: step(): centers = all_centers[block_lists]]
  transfers between devices with their start and end apart: 2 -> 2, of which waited for: 2 -> 2; matrix products, arithmetic and copies ran while one was open for 2% -> 3% of each run, Pallas kernels for 0% -> 0%
where the time goes in v1:
time: 184 us
  Pallas kernels  55.4 us (30%)
  waiting for transfers between devices  48.6 us (26%)
  blocking collectives  43.2 us (23%)
  between operations  14.3 us (8%)
  local copies, waits for them, and re-layouts  9.96 us (5%)
  other arithmetic  7.17 us (4%)
  matrix products  5.45 us (3%)
    pallas_call x1, Pallas kernels, partial_gradient(): pl.pallas_call(gradient_kernel, grid=(pairs,), in_specs=[pl.BlockSpec((po...  55.4 us
    psum x1, waiting for transfers between devices, local(): control_gradient = lax.psum(owned, ('fn', 'sub'))  29.3 us
    all_gather x2, blocking collectives, local(): lax.all_gather(adjoint.astype(jnp.bfloat16), 'node', axis=0, tiled=True)  28.1 us
    reduce_scatter x1, waiting for transfers between devices, local(): lax.psum_scatter(partial_value, 'node', scatter_dimension=0, tiled=True)  19.3 us
    all_gather x1, blocking collectives, local(): all_centers = lax.all_gather(control_coords, 'node', axis=0, tiled=True)  15.1 us
  transfers between devices with their start and end apart: 2, of which 2 were waited for; matrix products, arithmetic and copies ran while one was open for 3% of the time, Pallas kernels for 0%

profile of v1, /device:TPU:0, one launch (start us, length us, event | category | flops | bytes accessed | tf_op | source)
XLA Modules:
  0.0 184.1 jit_solution(11837700443615509189)
XLA Ops:
  7.2 15.1 %all_gather.9 = f32[32,3,128]{2,0,1:T(8,128)S(1)} all-gather(f32[8,3,128]{2,0,1:T(8,128)} %param.9), channel_id=1, replica_groups=mesh['sect'=2,'node'=4,'fn'=2,'sub'=2] {'node'}, dimensions={0}, use_global_device_ids=true | all-gather | bytes 61440 | tf_op jit(solution)/shard_map/all_gather | solution.py:102
  22.7 0.2 reshape.109.right_ref
  22.8 0.9 fusion.13
  24.1 2.1 %concatenate.13 = bf16[64,32,128]{2,1,0:T(8,128)(2,1)S(1)} concatenate(bf16[64,3,128]{2,1,0:T(4,128)(2,1)S(1)} %copy.90, bf16[64,3,128]{2,1,0:T(4,128)(2,1)S(1)} %copy.91, bf16[64,3,128]{2,1,0:T(4,128)(2,1)S(1)} %copy.90, bf16[64,3,128]{2,1,0:T(4,128)(2,1)S(1)} %copy.91, bf16[64,1,128]{2,1,0:T(2,128)(2,1)S(1)} %copy.94, bf16[64,1,128]{2,1,0:T(2,128)(2,1)S(1)} %copy.95, ...), dimensions={1} | concatenate | bytes 1048576 | tf_op jit(solution)/shard_map/concatenate | solution.py:47
  26.2 1.0 copy.97
  27.4 1.3 broadcast_in_dim.14
  28.7 2.9 %reshape.111.weight_ref = f32[16,2,8192]{2,1,0:T(2,128)} reshape(f32[32,64,128]{2,1,0:T(8,128)} %broadcast_in_dim.14) | data formatting | bytes 2097152 | tf_op jit(solution)/shard_map/reshape | solution.py:85
  31.6 1.2 copy-done.1
  32.8 55.4 %shard_map.77 = f32[32,32,128]{2,1,0:T(8,128)} custom-call(bf16[8192,32]{1,0:T(8,128)(2,1)S(1)} %bitcast.53, bf16[16,32,256]{2,1,0:T(8,128)(2,1)S(1)} %reshape.109.right_ref, bf16[32,8192]{1,0:T(8,128)(2,1)S(1)} %copy_bitcast_fusion.grad_ref, f32[16,2,8192]{2,1,0:T(2,128)S(1)} %copy-done.1), custom_call_target="tpu_custom_call" | custom-call | tf_op jit(solution)/shard_map/pallas_call | solution.py:86
  88.3 0.2 fusion.20
  88.6 3.4 %multiply_reduce_fusion = f32[8,4,128,128]{3,2,1,0:T(8,128)} fusion(f32[8,3,128]{2,1,0:T(4,128)S(1)} %copy.110, f32[8,4,3,128]{3,2,1,0:T(4,128)S(1)} %copy.109), kind=kLoop, calls=%fused_computation | loop fusion | flops 4194304 | bytes 2158592 | tf_op jit(solution)/shard_map/reduce_sum | solution.py:21
  92.0 19.3 %reduce-scatter.2.cloned.1.call-done = f32[8,32,128]{2,1,0:T(8,128)} async-done(((f32[32,32,128]{2,1,0:T(8,128)}), f32[8,32,128]{2,1,0:T(8,128)}) %reduce-scatter.2.cloned.1.call-update) | async-done | bytes 131088 | tf_op jit(solution)/shard_map/reduce_scatter | solution.py:104
  111.3 2.7 %multiply_convert_fusion = bf16[8,4,128,128]{3,2,1,0:T(8,128)(2,1)S(1)} fusion(f32[8,4,128,128]{3,2,1,0:T(8,128)} %multiply_reduce_fusion), kind=kLoop, calls=%fused_computation.1 | loop fusion | flops 4718592 | bytes 3145728 | tf_op jit(solution)/shard_map/convert_element_type | solution.py:24
  113.9 29.3 %all-reduce.2.cloned.1.call-done = f32[8,32,128]{2,1,0:T(8,128)} async-done(((f32[8,32,128]{2,1,0:T(8,128)}), f32[8,32,128]{2,1,0:T(8,128)}) %all-reduce.2.cloned.1.call-update) | async-done | bytes 131088 | tf_op jit(solution)/shard_map/psum | solution.py:105
  143.3 1.5 convolution_convert_fusion.1
  144.7 14.0 %all_gather.10 = bf16[32,32,128]{2,1,0:T(8,128)(2,1)S(1)} all-gather(bf16[8,32,128]{2,1,0:T(8,128)(2,1)S(1)} %convolution_convert_fusion.1), channel_id=1, replica_groups=mesh['sect'=2,'node'=4,'fn'=2,'sub'=2] {'node'}, dimensions={0}, use_global_device_ids=true | all-gather | bytes 327680 | tf_op jit(solution)/shard_map/all_gather | solution.py:116
  158.7 0.3 fusion.4
  159.0 1.2 fusion.1
  160.2 0.6 convolution_convert_fusion
  160.7 14.1 %all_gather.11 = bf16[32,32,128]{2,1,0:T(8,128)(2,1)S(1)} all-gather(bf16[8,32,128]{2,1,0:T(8,128)(2,1)S(1)} %convolution_convert_fusion), channel_id=1, replica_groups=mesh['sect'=2,'node'=4,'fn'=2,'sub'=2] {'node'}, dimensions={0}, use_global_device_ids=true | all-gather | bytes 327680 | tf_op jit(solution)/shard_map/all_gather | solution.py:116
  174.8 0.3 fusion.2
  175.1 0.3 fusion
  175.4 1.2 fusion.33
  176.6 0.7 copy.153
  (41 shorter events, 0.8 us)
Async XLA Ops:
  7.2 24.4 %copy-start = (bf16[64,32,128]{2,1,0:T(8,128)(2,1)S(1)}, bf16[64,32,128]{2,1,0:T(8,128)(2,1)}, u32[]{:S(2)}) copy-start(bf16[64,32,128]{2,1,0:T(8,128)(2,1)} %param.6) | copy-start | bytes 1572868
  7.2 104.1 %reduce-scatter.2.cloned.1.call-start = ((), (), s32[]{:S(2)}) async-start(), calls=%async_computation.1 | async-start | bytes 655360 | tf_op jit(solution)/shard_map/reduce_scatter | solution.py:104
  24.0 3.3 %copy-start.6 = (s32[64,32]{0,1:T(8,128)S(1)}, s32[64,32]{0,1:T(8,128)}, u32[]{:S(2)}) copy-start(s32[64,32]{0,1:T(8,128)} %param.8) | copy-start | bytes 24580
  31.6 1.2 copy-start.1
  32.8 55.4 %copy-start.4 = (f32[8,3,128]{2,0,1:T(8,128)S(1)}, f32[8,3,128]{2,0,1:T(8,128)}, u32[]{:S(2)}) copy-start(f32[8,3,128]{2,0,1:T(8,128)} %param.9) | copy-start | bytes 36868
  32.8 55.5 %copy-start.5 = (s32[8,4]{0,1:T(4,128)S(1)}, s32[8,4]{0,1:T(4,128)}, u32[]{:S(2)}) copy-start(s32[8,4]{0,1:T(4,128)} %param.10) | copy-start | bytes 388
  88.2 55.0 %all-reduce.2.cloned.1.call-start = ((), (), s32[]{:S(2)}) async-start(), calls=%async_computation.2 | async-start | bytes 262144 | tf_op jit(solution)/shard_map/psum | solution.py:105
  92.0 51.3 %copy-start.2 = (f32[8,128,128]{2,1,0:T(8,128)S(1)}, f32[8,128,128]{2,1,0:T(8,128)}, u32[]{:S(2)}) copy-start(f32[8,128,128]{2,1,0:T(8,128)} %param.11) | copy-start | bytes 1572868
  144.7 30.4 %copy-start.3 = (f32[8,32,128]{2,1,0:T(8,128)S(1)}, f32[8,32,128]{2,1,0:T(8,128)}, u32[]{:S(2)}) copy-start(f32[8,32,128]{2,1,0:T(8,128)} %all-reduce.2.cloned.1.call-done) | copy-start | bytes 393220
Sparse Core Ops, SparseCore 0:
  88.4 22.8 reduce-scatter.1
  113.6 29.6 all-reduce.1

commit v2 on v1

--- a/solution.py
+++ b/solution.py
@@ -14,6 +14,9 @@
 
 
 DEPTH = 32
+
+
+MESH = pl.DeviceIdType.MESH
 
 
 def wendland(points, centers):
@@ -98,36 +101,263 @@
     )(left, right, grads, weights)
 
 
-def local(volume_grad, volume_coords, support, control_coords, neighbours, block_inverse):
-    all_centers = lax.all_gather(control_coords, "node", axis=0, tiled=True)
+def place(rank, sizes):
+    copies = sizes[1] * sizes[2]
+    return {
+        "node": rank // copies,
+        "fn": (rank % copies) // sizes[2],
+        "sub": rank % sizes[2],
+    }
+
+
+def signal_and_wait(peers, where):
+    barrier = pltpu.get_barrier_semaphore()
+
+    def tell(step, carry):
+        pl.semaphore_signal(barrier, inc=1, device_id=where(step), device_id_type=MESH)
+        return carry
+
+    lax.fori_loop(1, peers + 1, tell, 0)
+    pl.semaphore_wait(barrier, peers)
+
+
+def center_kernel(nodes, own_ref, all_ref, send_sem, recv_sem):
+    me = lax.axis_index("node")
+
+    def where(step):
+        return {"node": (me + step) % nodes}
+
+    signal_and_wait(nodes - 1, where)
+    all_ref[me] = own_ref[...]
+
+    def copy(step):
+        return pltpu.make_async_remote_copy(
+            src_ref=own_ref,
+            dst_ref=all_ref.at[me],
+            send_sem=send_sem.at[step],
+            recv_sem=recv_sem.at[step],
+            device_id=where(step),
+            device_id_type=MESH,
+        )
+
+    for step in range(1, nodes):
+        copy(step).start()
+    for step in range(1, nodes):
+        copy(step).wait()
+
+
+def gather_centers(control_coords, nodes):
+    own, dims, width = control_coords.shape
+    gathered = pl.pallas_call(
+        functools.partial(center_kernel, nodes),
+        in_specs=[pl.BlockSpec(memory_space=pltpu.VMEM)],
+        out_specs=pl.BlockSpec(memory_space=pltpu.VMEM),
+        out_shape=jax.ShapeDtypeStruct((nodes, own * dims, width), jnp.float32),
+        scratch_shapes=[
+            pltpu.SemaphoreType.DMA((nodes,)),
+            pltpu.SemaphoreType.DMA((nodes,)),
+        ],
+        compiler_params=pltpu.CompilerParams(collective_id=0, has_side_effects=True),
+    )(control_coords.reshape(own * dims, width))
+    return gathered.reshape(nodes * own, dims, width)
+
+
+def adjoint_kernel(
+    sizes,
+    near_ref,
+    part_ref,
+    inverse_ref,
+    phi_ref,
+    gradient_ref,
+    adjoint_ref,
+    landed,
+    values,
+    wide,
+    total,
+    part_send,
+    part_recv,
+    gradient_send,
+    gradient_recv,
+    adjoint_send,
+    adjoint_recv,
+    value_send,
+    value_recv,
+):
+    nodes = sizes[0]
+    copies = sizes[1] * sizes[2]
+    ranks = nodes * copies
+    node = lax.axis_index("node")
+    share = lax.axis_index("fn") * sizes[2] + lax.axis_index("sub")
+    rank = node * copies + share
+    own = inverse_ref.shape[0]
+    rows = part_ref.shape[1] // own
+    coupled = phi_ref.shape[1] // phi_ref.shape[2]
+    width = phi_ref.shape[2]
+
+    def peer(step):
+        return (rank + step) % ranks
+
+    signal_and_wait(ranks - 1, lambda step: place(peer(step), sizes))
+
+    def part_copy(step):
+        return pltpu.make_async_remote_copy(
+            src_ref=part_ref.at[peer(step)],
+            dst_ref=landed.at[step],
+            send_sem=part_send.at[step],
+            recv_sem=part_recv.at[step],
+            device_id=place(peer(step), sizes),
+            device_id_type=MESH,
+        )
+
+    def start_part(step, carry):
+        part_copy(step).start()
+        return carry
+
+    lax.fori_loop(1, ranks, start_part, 0)
+    total[...] = part_ref[rank].astype(jnp.float32)
+
+    def add_part(step, carry):
+        part_copy(step).wait_recv()
+        total[...] += landed[step].astype(jnp.float32)
+        return carry
+
+    lax.fori_loop(1, ranks, add_part, 0)
+    gradient_ref[share] = total[...]
+
+    def share_copy(ref, send, recv, step):
+        return pltpu.make_async_remote_copy(
+            src_ref=ref.at[share],
+            dst_ref=ref.at[share],
+            send_sem=send.at[step],
+            recv_sem=recv.at[step],
+            device_id=place(node * copies + (share + step) % copies, sizes),
+            device_id_type=MESH,
+        )
+
+    for step in range(1, copies):
+        share_copy(gradient_ref, gradient_send, gradient_recv, step).start()
+
+    def solve(c, coupling):
+        right = total[c * rows : (c + 1) * rows, :]
+        if coupling is not None:
+            right = right - coupling
+        return jnp.dot(
+            right,
+            inverse_ref[c],
+            precision=lax.Precision.HIGHEST,
+            preferred_element_type=jnp.float32,
+        )
+
+    def value_copy(sweep, step):
+        return pltpu.make_async_remote_copy(
+            src_ref=values.at[sweep, node],
+            dst_ref=values.at[sweep, node],
+            send_sem=value_send.at[sweep, step],
+            recv_sem=value_recv.at[sweep, step],
+            device_id=place(((node + step) % nodes) * copies + share, sizes),
+            device_id_type=MESH,
+        )
+
+    adjoint = [solve(c, None) for c in range(own)]
+    for sweep in range(SWEEPS):
+        values[sweep, node] = jnp.concatenate(adjoint, 0).astype(jnp.bfloat16)
+        for step in range(1, nodes):
+            value_copy(sweep, step).start()
+        for step in range(1, nodes):
+            value_copy(sweep, step).wait_recv()
+        for n in range(nodes):
+            block = values[sweep, n].astype(jnp.float32)
+            wide[n * own : (n + 1) * own] = block.reshape(own, rows, width)
+        adjoint = []
+        for c in range(own):
+            near = [wide[near_ref[c, k]] for k in range(coupled)]
+            near = jnp.concatenate(near, 1).astype(jnp.bfloat16)
+            coupling = jnp.dot(near, phi_ref[c], preferred_element_type=jnp.float32)
+            adjoint.append(solve(c, coupling))
+    adjoint_ref[share] = jnp.concatenate(adjoint, 0)
+    for step in range(1, copies):
+        share_copy(adjoint_ref, adjoint_send, adjoint_recv, step).start()
+
+    def end_part(step, carry):
+        part_copy(step).wait_send()
+        return carry
+
+    lax.fori_loop(1, ranks, end_part, 0)
+    for sweep in range(SWEEPS):
+        for step in range(1, nodes):
+            value_copy(sweep, step).wait_send()
+    for step in range(1, copies):
+        share_copy(gradient_ref, gradient_send, gradient_recv, step).wait()
+    for step in range(1, copies):
+        share_copy(adjoint_ref, adjoint_send, adjoint_recv, step).wait()
+
+
+def sum_and_solve(parts, neighbours, block_inverse, pair_phi, sizes):
+    nodes = sizes[0]
+    copies = sizes[1] * sizes[2]
+    ranks, height, width = parts.shape
+    own = block_inverse.shape[0]
+    rows = height // own
+    vmem = pl.BlockSpec(memory_space=pltpu.VMEM)
+    dma = pltpu.SemaphoreType.DMA
+    return pl.pallas_call(
+        functools.partial(adjoint_kernel, sizes),
+        in_specs=[pl.BlockSpec(memory_space=pltpu.SMEM), vmem, vmem, vmem],
+        out_specs=[vmem, vmem],
+        out_shape=[jax.ShapeDtypeStruct((copies, height, width), jnp.float32)] * 2,
+        scratch_shapes=[
+            pltpu.VMEM((ranks, height, width), jnp.bfloat16),
+            pltpu.VMEM((SWEEPS, nodes, height, width), jnp.bfloat16),
+            pltpu.VMEM((nodes * own, rows, width), jnp.float32),
+            pltpu.VMEM((height, width), jnp.float32),
+            dma((ranks,)),
+            dma((ranks,)),
+            dma((copies,)),
+            dma((copies,)),
+            dma((copies,)),
+            dma((copies,)),
+            dma((SWEEPS, nodes)),
+            dma((SWEEPS, nodes)),
+        ],
+        compiler_params=pltpu.CompilerParams(
+            collective_id=1, has_side_effects=True, vmem_limit_bytes=40 << 20
+        ),
+    )(neighbours, parts, block_inverse, pair_phi)
+
+
+def local(
+    sizes, volume_grad, volume_coords, support, control_coords, neighbours, block_inverse
+):
+    nodes = sizes[0]
+    copies = sizes[1] * sizes[2]
+    own, coupled = neighbours.shape
+    funcs, width = volume_grad.shape[1:]
+    taken = funcs // copies
+    rows = max(taken, 8)
+    all_centers = gather_centers(control_coords, nodes)
     partial_value = partial_gradient(volume_grad, volume_coords, support, all_centers)
-    owned = lax.psum_scatter(partial_value, "node", scatter_dimension=0, tiled=True)
-    control_gradient = lax.psum(owned, ("fn", "sub"))
-    adjoint = jnp.einsum(
-        "cfi,cij->cfj", control_gradient, block_inverse, precision=lax.Precision.HIGHEST
-    )
+    parts = partial_value.reshape(nodes, own, copies, taken, width).transpose(0, 2, 1, 3, 4)
+    parts = jnp.pad(parts, ((0, 0),) * 3 + ((0, rows - taken), (0, 0)))
+    parts = parts.reshape(nodes * copies, own * rows, width).astype(jnp.bfloat16)
     picks = neighbours[:, :, None] == jnp.arange(all_centers.shape[0], dtype=jnp.int32)
     near_coords = jnp.einsum(
         "ckn,ndi->ckdi", picks.astype(jnp.float32), all_centers, precision=lax.Precision.HIGHEST
     )
     pair_phi = wendland(near_coords, control_coords[:, None])
-    picks = picks.astype(jnp.bfloat16)
-    for sweep in range(SWEEPS):
-        values = lax.all_gather(adjoint.astype(jnp.bfloat16), "node", axis=0, tiled=True)
-        near = jnp.einsum("ckn,nfi->ckfi", picks, values)
-        coupling = jnp.einsum("ckfi,ckij->cfj", near, pair_phi, preferred_element_type=jnp.float32)
-        adjoint = jnp.einsum(
-            "cfi,cij->cfj",
-            control_gradient - coupling,
-            block_inverse,
-            precision=lax.Precision.HIGHEST,
-        )
-    return (control_gradient, adjoint)
+    pair_phi = pair_phi.reshape(own, coupled * width, width)
+    outputs = sum_and_solve(parts, neighbours, block_inverse, pair_phi, sizes)
+
+    def whole(shares):
+        shares = shares.reshape(copies, own, rows, width)[:, :, :taken]
+        return shares.transpose(1, 0, 2, 3).reshape(own, funcs, width)
+
+    return tuple(whole(shares) for shares in outputs)
 
 
 def solution(mesh):
+    sizes = tuple(mesh.shape[name] for name in ("node", "fn", "sub"))
     return jax.shard_map(
-        local,
+        functools.partial(local, sizes),
         mesh=mesh,
         in_specs=(
             P(("sect", "node", "fn", "sub"), None, None),

time: 184 us -> 109 us (0.59)
  waiting for transfers between devices: 48.6 us -> 0 us
  blocking collectives: 43.2 us -> 0 us
  Pallas kernels: 55.4 us -> 89.5 us
  between operations: 14.3 us -> 0.94 us
  matrix products: 5.45 us -> 0.21 us
  local copies, waits for them, and re-layouts: 9.96 us -> 12.4 us
  other arithmetic: 7.17 us -> 5.14 us
    all_gather x3 -> x0, blocking collectives: 43.2 us -> none  [the longest x2 28.1 us: local(): lax.all_gather(adjoint.astype(jnp.bfloat16), 'node', axis=0, tiled=True)]
    pallas_call x0 -> x2, Pallas kernels: none -> 34.7 us  [the longest x1 25.9 us: sum_and_solve(): pl.pallas_call(functools.partial(adjoint_kernel, sizes), in_specs=[pl.Blo...]
    psum x1 -> x0, waiting for transfers between devices: 29.3 us -> none  [local(): control_gradient = lax.psum(owned, ('fn', 'sub'))]
    reduce_scatter x1 -> x0, waiting for transfers between devices: 19.3 us -> none  [local(): lax.psum_scatter(partial_value, 'node', scatter_dimension=0, tiled=True)]
    dot_general x7 -> x0, matrix products: 5.24 us -> none  [the longest x2 1.79 us: local(): jnp.einsum('cfi,cij->cfj', control_gradient - coupling, block_inverse, pr...]
    reshape x0 -> x3, local copies, waits for them, and re-layouts: none -> 2.16 us  [the longest x1 0.82 us: gather_centers(): return gathered.reshape(nodes * own, dims, width)]
  transfers between devices with their start and end apart: 2 -> 0, of which waited for: 2 -> 0; matrix products, arithmetic and copies ran while one was open for 3% -> 0% of each run, Pallas kernels for 0% -> 0%
where the time goes in v2:
time: 109 us; the launch traced here: 108 us
  Pallas kernels  89.5 us (82%)
  local copies, waits for them, and re-layouts  12.4 us (11%)
  other arithmetic  5.14 us (5%)
    pallas_call x1, Pallas kernels, partial_gradient(): pl.pallas_call(gradient_kernel, grid=(pairs,), in_specs=[pl.BlockSpec((po...  54.7 us
    pallas_call x1, Pallas kernels, sum_and_solve(): pl.pallas_call(functools.partial(adjoint_kernel, sizes), in_specs=[pl.Blo...  25.9 us
    pallas_call x1, Pallas kernels, gather_centers(): pl.pallas_call(functools.partial(center_kernel, nodes), in_specs=[pl.Bloc...  8.83 us
    reshape x1, local copies, waits for them, and re-layouts, partial_gradient(): weights = weights.reshape(pairs, 2, points)  2.86 us
    unnamed x20, local copies, waits for them, and re-layouts  2.28 us
    concatenate x2, local copies, waits for them, and re-layouts, factors(): return jnp.concatenate(rows, axis=1).astype(jnp.bfloat16)  2.19 us

profile of v2, /device:TPU:0, one launch (start us, length us, event | category | flops | bytes accessed | tf_op | source)
XLA Modules:
  0.0 108.1 jit_solution(4559766753916879736)
XLA Ops:
  0.6 0.0 copy-start
  0.6 0.8 copy.116
  1.4 0.6 reshape.148.own_ref
  2.0 8.8 %shard_map.77 = f32[4,24,128]{2,1,0:T(8,128)} custom-call(f32[24,128]{1,0:T(8,128)} %reshape.148.own_ref), custom_call_target="tpu_custom_call" | custom-call | tf_op jit(solution)/shard_map/pallas_call | solution.py:151
  10.9 0.8 broadcast_multiply_fusion
  11.9 0.8 reshape.149
  12.7 0.1 fusion.6
  12.9 0.1 broadcast_dynamic-update-slice_fusion
  12.9 0.2 reshape.150.right_ref
  13.1 0.9 fusion.3
  14.4 2.1 %concatenate.9 = bf16[64,32,128]{2,1,0:T(8,128)(2,1)S(1)} concatenate(bf16[64,3,128]{2,1,0:T(4,128)(2,1)S(1)} %copy.108, bf16[64,3,128]{2,1,0:T(4,128)(2,1)S(1)} %copy.109, bf16[64,3,128]{2,1,0:T(4,128)(2,1)S(1)} %copy.108, bf16[64,3,128]{2,1,0:T(4,128)(2,1)S(1)} %copy.109, bf16[64,1,128]{2,1,0:T(2,128)(2,1)S(1)} %copy.112, bf16[64,1,128]{2,1,0:T(2,128)(2,1)S(1)} %copy.113, ...), dimensions={1} | concatenate | bytes 1048576 | tf_op jit(solution)/shard_map/concatenate | solution.py:50
  16.5 1.0 copy.115
  17.6 0.1 convert_reduce_fusion
  17.7 1.3 %broadcast_in_dim.14 = f32[32,64,128]{2,1,0:T(8,128)} broadcast(f32[32,64]{1,0:T(8,128)S(1)} %broadcast_multiply_fusion.1), dimensions={0,1} | broadcast | bytes 1056768 | tf_op jit(solution)/shard_map/broadcast_in_dim | solution.py:87
  19.0 2.9 %reshape.152.weight_ref = f32[16,2,8192]{2,1,0:T(2,128)} reshape(f32[32,64,128]{2,1,0:T(8,128)} %broadcast_in_dim.14) | data formatting | bytes 2097152 | tf_op jit(solution)/shard_map/reshape | solution.py:88
  21.9 1.2 %copy-done.1 = f32[16,2,8192]{2,1,0:T(2,128)S(1)} copy-done((f32[16,2,8192]{2,1,0:T(2,128)S(1)}, f32[16,2,8192]{2,1,0:T(2,128)}, u32[]{:S(2)}) %copy-start.1) | copy-done | bytes 1048600
  23.1 54.7 %shard_map.78 = f32[32,32,128]{2,1,0:T(8,128)S(1)} custom-call(bf16[8192,32]{1,0:T(8,128)(2,1)S(1)} %bitcast.44, bf16[16,32,256]{2,1,0:T(8,128)(2,1)S(1)} %reshape.150.right_ref, bf16[32,8192]{1,0:T(8,128)(2,1)S(1)} %copy_bitcast_fusion.grad_ref, f32[16,2,8192]{2,1,0:T(2,128)S(1)} %copy-done.1), custom_call_target="tpu_custom_call" | custom-call | tf_op jit(solution)/shard_map/pallas_call | solution.py:89
  77.9 0.1 copy.129
  78.0 0.2 fusion.11
  78.2 2.1 %multiply_reduce_fusion = f32[8,4,128,128]{3,2,1,0:T(8,128)S(1)} fusion(f32[8,3,128]{2,1,0:T(4,128)S(1)} %copy.116, f32[8,4,3,128]{3,2,1,0:T(4,128)S(1)} %copy.131), kind=kLoop, calls=%fused_computation | loop fusion | flops 4194304 | bytes 2158592 | tf_op jit(solution)/shard_map/reduce_sum | solution.py:24
  80.3 1.1 %multiply_convert_fusion = bf16[8,4,128,128]{3,2,1,0:T(8,128)(2,1)S(1)} fusion(f32[8,4,128,128]{3,2,1,0:T(8,128)S(1)} %multiply_reduce_fusion), kind=kLoop, calls=%fused_computation.1 | loop fusion | flops 4718592 | bytes 3145728 | tf_op jit(solution)/shard_map/convert_element_type | solution.py:27
  81.4 0.1 copy.133.near_ref
  81.5 25.9 %shard_map.79 = (f32[4,64,128]{2,1,0:T(8,128)S(1)}, f32[4,64,128]{2,1,0:T(8,128)S(1)}) custom-call(s32[8,4]{1,0:T(8,128)S(1)} %copy.133.near_ref, bf16[16,64,128]{2,1,0:T(8,128)(2,1)S(1)} %bitcast.46, f32[8,128,128]{2,1,0:T(8,128)S(1)} %copy-done.2, bf16[8,512,128]{2,1,0:T(8,128)(2,1)S(1)} %bitcast.45), custom_call_target="tpu_custom_call" | custom-call | tf_op jit(solution)/shard_map/pallas_call | solution.py:303
  107.4 0.7 copy_bitcast_fusion.1
  (31 shorter events, 0.6 us)
Async XLA Ops:
  0.6 21.2 %copy-start = (bf16[64,32,128]{2,1,0:T(8,128)(2,1)S(1)}, bf16[64,32,128]{2,1,0:T(8,128)(2,1)}, u32[]{:S(2)}) copy-start(bf16[64,32,128]{2,1,0:T(8,128)(2,1)} %param.6) | copy-start | bytes 1572868
  14.3 3.3 %copy-start.3 = (s32[64,32]{0,1:T(8,128)S(1)}, s32[64,32]{0,1:T(8,128)}, u32[]{:S(2)}) copy-start(s32[64,32]{0,1:T(8,128)} %param.8) | copy-start | bytes 24580
  21.9 1.2 %copy-start.1 = (f32[16,2,8192]{2,1,0:T(2,128)S(1)}, f32[16,2,8192]{2,1,0:T(2,128)}, u32[]{:S(2)}) copy-start(f32[16,2,8192]{2,1,0:T(2,128)} %reshape.152.weight_ref) | copy-start | bytes 3145732
  23.1 54.9 %copy-start.4 = (s32[8,4]{0,1:T(4,128)S(1)}, s32[8,4]{0,1:T(4,128)}, u32[]{:S(2)}) copy-start(s32[8,4]{0,1:T(4,128)} %param.10) | copy-start | bytes 388
  80.3 1.2 %copy-start.2 = (f32[8,128,128]{2,1,0:T(8,128)S(1)}, f32[8,128,128]{2,1,0:T(8,128)}, u32[]{:S(2)}) copy-start(f32[8,128,128]{2,1,0:T(8,128)} %inverse_ref.1) | copy-start | bytes 1572868

commit v3 on v2

--- a/solution.py
+++ b/solution.py
@@ -14,6 +14,12 @@
 
 
 DEPTH = 32
+
+
+ROUND_UP = 1.0 + 2.0**-19
+
+
+TINY = 1e-12
 
 
 MESH = pl.DeviceIdType.MESH
@@ -39,7 +45,8 @@
 def factors(points, left):
     high, low = cut(points * (1.0 / RADIUS), 2)
     kept = high + low
-    norm = jnp.concatenate(cut(jnp.sum(kept * kept, axis=1, keepdims=True), 3), axis=1)
+    norm = jnp.sum(kept * kept, axis=1, keepdims=True) * ROUND_UP + TINY
+    norm = jnp.concatenate(cut(norm, 3), axis=1)
     one = jnp.ones_like(norm)
     if left:
         rows = [high, low, high, low, norm, one]
@@ -51,32 +58,44 @@
 
 
 def quarter_phi(square):
-    square = jnp.maximum(square, 1e-12)
     ratio = square * lax.rsqrt(square)
     inside = jnp.maximum(1.0 - ratio, 0.0)
     inside = inside * inside
     return (inside * inside * (ratio + 0.25)).astype(jnp.bfloat16)
 
 
-def gradient_kernel(left_ref, right_ref, grad_ref, weight_ref, out_ref):
+def gradient_kernel(left_ref, right_ref, grad_ref, count_ref, out_ref, weight_ref):
     funcs = grad_ref.shape[0]
     width = out_ref.shape[2]
-    square = jnp.dot(left_ref[...], right_ref[0], preferred_element_type=jnp.float32)
-    phi = quarter_phi(square)
-    grads = grad_ref[...]
-    scaled = []
-    for half in range(2):
-        row = jnp.broadcast_to(weight_ref[0, half : half + 1, :], grads.shape)
-        scaled.append(grads * row.astype(jnp.bfloat16))
-    both = jnp.dot(jnp.concatenate(scaled, 0), phi, preferred_element_type=jnp.float32)
-    out_ref[0] = both[:funcs, :width]
-    out_ref[1] = both[funcs:, width:]
+    pairs = right_ref.shape[0]
+
+    @pl.when(pl.program_id(0) == 0)
+    def _():
+        for s in range(count_ref.shape[1]):
+            column = count_ref[:, s : s + 1]
+            weight_ref[:, s * width : (s + 1) * width] = jnp.broadcast_to(
+                column, (column.shape[0], width)
+            )
+
+    for pair in range(pairs):
+        square = jnp.dot(left_ref[...], right_ref[pair], preferred_element_type=jnp.float32)
+        phi = quarter_phi(square)
+        grads = grad_ref[...]
+        scaled = []
+        for half in range(2):
+            row = weight_ref[pl.ds((pl.program_id(0) * pairs + pair) * 2 + half, 1), :]
+            row = jnp.broadcast_to(row, grads.shape)
+            scaled.append(grads * row.astype(jnp.bfloat16))
+        both = jnp.dot(jnp.concatenate(scaled, 0), phi, preferred_element_type=jnp.float32)
+        out_ref[2 * pair] = both[:funcs, :width]
+        out_ref[2 * pair + 1] = both[funcs:, width:]
 
 
 def partial_gradient(volume_grad, volume_coords, support, all_centers):
     blocks, funcs, width = volume_grad.shape
     control = all_centers.shape[0]
     pairs = control // 2
+    together = next(n for n in (4, 2, 1) if pairs % n == 0)
     points = blocks * width
     left = factors(volume_coords, True).transpose(0, 2, 1).reshape(points, DEPTH)
     right = factors(all_centers, False).reshape(pairs, 2, DEPTH, width)
@@ -84,21 +103,20 @@
     grads = volume_grad.transpose(1, 0, 2).reshape(funcs, points)
     listed = support[None] == jnp.arange(control, dtype=jnp.int32)[:, None, None]
     counts = 4.0 * jnp.sum(listed.astype(jnp.float32), axis=2)
-    weights = jnp.broadcast_to(counts[:, :, None], (control, blocks, width))
-    weights = weights.reshape(pairs, 2, points)
     return pl.pallas_call(
         gradient_kernel,
-        grid=(pairs,),
+        grid=(pairs // together,),
         in_specs=[
             pl.BlockSpec((points, DEPTH), lambda i: (0, 0)),
-            pl.BlockSpec((1, DEPTH, 2 * width), lambda i: (i, 0, 0)),
+            pl.BlockSpec((together, DEPTH, 2 * width), lambda i: (i, 0, 0)),
             pl.BlockSpec((funcs, points), lambda i: (0, 0)),
-            pl.BlockSpec((1, 2, points), lambda i: (i, 0, 0)),
+            pl.BlockSpec((control, blocks), lambda i: (0, 0)),
         ],
-        out_specs=pl.BlockSpec((2, funcs, width), lambda i: (i, 0, 0)),
+        out_specs=pl.BlockSpec((2 * together, funcs, width), lambda i: (i, 0, 0)),
         out_shape=jax.ShapeDtypeStruct((control, funcs, width), jnp.float32),
+        scratch_shapes=[pltpu.VMEM((control, points), jnp.float32)],
         compiler_params=pltpu.CompilerParams(vmem_limit_bytes=48 << 20),
-    )(left, right, grads, weights)
+    )(left, right, grads, counts)
 
 
 def place(rank, sizes):

time: 109 us -> 91.5 us (0.84)
  Pallas kernels: 89.5 us -> 77.7 us
  local copies, waits for them, and re-layouts: 12.4 us -> 6.99 us
    pallas_call x1, Pallas kernels: 54.7 us -> 43 us  [partial_gradient(): pl.pallas_call(gradient_kernel, grid=(pairs // together,), in_specs=[pl.B...]
    reshape x1 -> x0, local copies, waits for them, and re-layouts: 2.86 us -> none  [partial_gradient(): weights = weights.reshape(pairs, 2, points)]
    broadcast_in_dim x1 -> x0, local copies, waits for them, and re-layouts: 1.33 us -> none  [partial_gradient(): weights = jnp.broadcast_to(counts[:, :, None], (control, blocks, width))]
    unnamed x20 -> x18, local copies, waits for them, and re-layouts: 2.28 us -> 1.06 us
where the time goes in v3:
time: 91.5 us; the launch traced here: 91.2 us
  Pallas kernels  77.7 us (85%)
  local copies, waits for them, and re-layouts  6.99 us (8%)
  other arithmetic  5.37 us (6%)
  between operations  0.95 us (1%)
    pallas_call x1, Pallas kernels, partial_gradient(): pl.pallas_call(gradient_kernel, grid=(pairs // together,), in_specs=[pl.B...  43 us
    pallas_call x1, Pallas kernels, sum_and_solve(): pl.pallas_call(functools.partial(adjoint_kernel, sizes), in_specs=[pl.Blo...  25.9 us
    pallas_call x1, Pallas kernels, gather_centers(): pl.pallas_call(functools.partial(center_kernel, nodes), in_specs=[pl.Bloc...  8.83 us
    reduce_sum x1, other arithmetic, wendland(): dist = jnp.sqrt(jnp.sum(diff * diff, axis=-3))  2.28 us
    concatenate x2, local copies, waits for them, and re-layouts, factors(): return jnp.concatenate(rows, axis=1).astype(jnp.bfloat16)  2.19 us

profile of v3, /device:TPU:0, one launch (start us, length us, event | category | flops | bytes accessed | tf_op | source)
XLA Modules:
  0.0 91.2 jit_solution(8833098766606494158)
XLA Ops:
  0.6 0.0 copy-start
  0.6 0.8 copy.116
  1.4 0.6 reshape.160.own_ref
  2.0 8.8 %shard_map.77 = f32[4,24,128]{2,1,0:T(8,128)} custom-call(f32[24,128]{1,0:T(8,128)} %reshape.160.own_ref), custom_call_target="tpu_custom_call" | custom-call | tf_op jit(solution)/shard_map/pallas_call | solution.py:169
  10.9 0.8 broadcast_multiply_fusion
  11.9 0.8 reshape.161
  12.7 0.1 fusion.6
  12.9 0.1 broadcast_dynamic-update-slice_fusion
  13.0 0.2 reshape.162.right_ref
  13.1 0.9 %fusion.3 = (f32[64,128]{1,0:T(8,128)S(1)}, bf16[64,3,128]{2,0,1:T(8,128)(2,1)S(1)}, bf16[64,3,128]{2,0,1:T(8,128)(2,1)S(1)}) fusion(f32[64,3,128]{2,0,1:T(8,128)} %param.7), kind=kLoop, calls=%fused_computation.13 | loop fusion | flops 212992 | bytes 229376 | tf_op jit(solution)/shard_map/reduce_sum | solution.py:48
  14.4 2.1 %concatenate.9 = bf16[64,32,128]{2,1,0:T(8,128)(2,1)S(1)} concatenate(bf16[64,3,128]{2,1,0:T(4,128)(2,1)S(1)} %copy.108, bf16[64,3,128]{2,1,0:T(4,128)(2,1)S(1)} %copy.109, bf16[64,3,128]{2,1,0:T(4,128)(2,1)S(1)} %copy.108, bf16[64,3,128]{2,1,0:T(4,128)(2,1)S(1)} %copy.109, bf16[64,1,128]{2,1,0:T(2,128)(2,1)S(1)} %copy.112, bf16[64,1,128]{2,1,0:T(2,128)(2,1)S(1)} %copy.113, ...), dimensions={1} | concatenate | bytes 1048576 | tf_op jit(solution)/shard_map/concatenate | solution.py:57
  16.5 0.0 copy-start.2
  16.5 1.0 %copy.115 = bf16[64,128,32]{2,1,0:T(8,128)(2,1)S(1)} copy(bf16[64,128,32]{1,2,0:T(8,128)(2,1)S(1)} %bitcast.47) | data formatting | bytes 1048576 | tf_op jit(solution)/shard_map/transpose | solution.py:100
  17.6 0.1 convert_reduce_fusion
  17.7 0.0 copy-start.3
  17.8 43.0 %shard_map.78 = f32[32,32,128]{2,1,0:T(8,128)S(1)} custom-call(bf16[8192,32]{1,0:T(8,128)(2,1)S(1)} %bitcast.44, bf16[16,32,256]{2,1,0:T(8,128)(2,1)S(1)} %reshape.162.right_ref, bf16[32,8192]{1,0:T(8,128)(2,1)S(1)} %copy_bitcast_fusion.grad_ref, f32[32,64]{1,0:T(8,128)S(1)} %broadcast_multiply_fusion.1.count_ref), custom_call_target="tpu_custom_call" | custom-call | tf_op jit(solution)/shard_map/pallas_call | solution.py:106
  60.8 0.1 copy.129
  60.9 0.2 fusion.11
  61.1 2.3 %multiply_reduce_fusion = f32[8,4,128,128]{3,2,1,0:T(8,128)S(1)} fusion(f32[8,3,128]{2,1,0:T(4,128)S(1)} %copy.116, f32[8,4,3,128]{3,2,1,0:T(4,128)S(1)} %copy.131), kind=kLoop, calls=%fused_computation | loop fusion | flops 4194304 | bytes 2158592 | tf_op jit(solution)/shard_map/reduce_sum | solution.py:30
  63.4 0.0 copy-start.1
  63.4 1.1 %multiply_convert_fusion = bf16[8,4,128,128]{3,2,1,0:T(8,128)(2,1)S(1)} fusion(f32[8,4,128,128]{3,2,1,0:T(8,128)S(1)} %multiply_reduce_fusion), kind=kLoop, calls=%fused_computation.1 | loop fusion | flops 4718592 | bytes 3145728 | tf_op jit(solution)/shard_map/convert_element_type | solution.py:33
  64.5 0.1 copy.133.near_ref
  64.6 25.9 %shard_map.79 = (f32[4,64,128]{2,1,0:T(8,128)S(1)}, f32[4,64,128]{2,1,0:T(8,128)S(1)}) custom-call(s32[8,4]{1,0:T(8,128)S(1)} %copy.133.near_ref, bf16[16,64,128]{2,1,0:T(8,128)(2,1)S(1)} %bitcast.46, f32[8,128,128]{2,1,0:T(8,128)S(1)} %copy-done.1, bf16[8,512,128]{2,1,0:T(8,128)(2,1)S(1)} %bitcast.45), custom_call_target="tpu_custom_call" | custom-call | tf_op jit(solution)/shard_map/pallas_call | solution.py:321
  90.5 0.7 copy_bitcast_fusion.1
  (28 shorter events, 0.6 us)
Async XLA Ops:
  0.6 16.9 %copy-start = (bf16[64,32,128]{2,1,0:T(8,128)(2,1)S(1)}, bf16[64,32,128]{2,1,0:T(8,128)(2,1)}, u32[]{:S(2)}) copy-start(bf16[64,32,128]{2,1,0:T(8,128)(2,1)} %param.6) | copy-start | bytes 1572868
  16.5 1.1 %copy-start.2 = (s32[64,32]{0,1:T(8,128)S(1)}, s32[64,32]{0,1:T(8,128)}, u32[]{:S(2)}) copy-start(s32[64,32]{0,1:T(8,128)} %param.8) | copy-start | bytes 24580
  17.7 43.1 %copy-start.3 = (s32[8,4]{0,1:T(4,128)S(1)}, s32[8,4]{0,1:T(4,128)}, u32[]{:S(2)}) copy-start(s32[8,4]{0,1:T(4,128)} %param.10) | copy-start | bytes 388
  63.4 1.2 %copy-start.1 = (f32[8,128,128]{2,1,0:T(8,128)S(1)}, f32[8,128,128]{2,1,0:T(8,128)}, u32[]{:S(2)}) copy-start(f32[8,128,128]{2,1,0:T(8,128)} %inverse_ref.1) | copy-start | bytes 1572868
